TPU v7x, 512 devices: a whole 4x8x8 slice. The times are simulated.
512 devices in a mesh: ibpa: 8 (over y), dom: 64 (over z, x, core).
Axes of the slice: x: 4, y: 8, z: 8, core: 2. Of those that a mesh axis runs over, the one named last changes fastest.
Arguments:
- initial_state: float32 [80, 8, 256, 512], P('ibpa', None, 'dom'), parts along dimension 0, may hold values from -6 to 6
- source: float32 [80, 8, 256, 512], P('ibpa', None, 'dom'), parts along dimension 0, may hold values from -6 to 6
- field_coupling: float32 [5, 5], replicated, may hold values from -2.5 to 2.5
- frequency: float32 [1], replicated, may hold values from 0.5 to 2
- phase_angle: float32 [8], P('ibpa'), parts along dimension 0, may hold values from -3.140625 to 3.140625
- face_owner: int32 [4096, 1], P('dom'), may hold values from 0 to 63; in each aligned block of 64 rows (0 to 63, 64 to 127, ...) at most 2 rows name the same one
- face_slot: int32 [4096], P('dom'), may hold values from 0 to 31
- radial_basis: float32 [256, 256], replicated, may hold values from -0.375 to 0.375
- cycle_coupling: float32 [2, 5, 5], replicated, may hold values from -2.5 to 2.5
- cycle_gain: float32 [2, 5, 256, 512], P(None, None, None, 'dom'), may hold values from 0.05 to 1
Outputs:
- relaxed: float32 [80, 8, 256, 512], P('ibpa', None, 'dom'), parts along dimension 0
- residual: float32 [80, 8, 256, 512], P('ibpa', None, 'dom'), parts along dimension 0
There are 8 independent parts, one for each index of `ibpa`. A program takes and returns all parts, laid end to end along the dimension named above; an argument that names none is the same for every part. Nothing has to cross between parts.
Inputs may be any that keep to these rules, and one draw needn't show every extreme that they name: `face_owner`: among the 64 faces of one device no owner rank appears more than 2 times, and in some device one appears exactly 2 times.
All inputs are finite; a program needn't handle non-finite values.
Results may differ from a plain program's by a relative error of at most 0.0001.
Values sent between devices are 32-bit elements; how exact they have to be, the bound alone decides.
A program may use at most 64 MiB of HBM per device.

v0:
```python
import functools

import jax
import jax.numpy as jnp
import ml_dtypes
import numpy as np
from jax import lax
from jax.experimental import pallas as pl
from jax.experimental.pallas import tpu as pltpu

F32 = jnp.float32
BF16 = jnp.bfloat16
AX = 8
RD = 4
MODES = 8
LINE = 80
OWN = LINE
PAD = 24
UPPER = OWN + RD * LINE + PAD
ROWS = UPPER + LINE
MESH = pl.DeviceIdType.MESH


@functools.lru_cache(None)
def fourier_tables(count):
    azi = MODES * count
    quarter = azi // 4
    kk, e = np.arange(quarter) // count, np.arange(quarter) % count
    k = 2 * e + kk
    t = np.arange(quarter)
    ahead, back = [], []
    for b in range(4):
        angle = ((4 * k + b)[:, None] * t[None, :]) % azi * (2 * np.pi / azi)
        ahead.append(np.concatenate([np.cos(angle), np.sin(angle)], axis=1))
        back.append(np.concatenate([np.cos(angle), np.sin(angle)], axis=0) / azi)

    def split(x):
        x = x.astype(np.float32)
        hi = x.astype(ml_dtypes.bfloat16)
        lo = (x - hi.astype(np.float32)).astype(ml_dtypes.bfloat16)
        return np.stack([hi, lo])

    return split(np.stack(ahead)), split(np.stack(back))


def split(x):
    hi = x.astype(BF16)
    return hi, (x - hi.astype(F32)).astype(BF16)


def dot3(a, b, contract=((1,), (0,))):
    dims = (contract, ((), ()))

    def one(u, v):
        return lax.dot_general(u, v, dims, preferred_element_type=F32)

    return one(a[0], b[0]) + (one(a[1], b[0]) + one(a[0], b[1]))


def get(ref, rows):
    return jnp.concatenate([ref[tile, rows, :] for tile in range(ref.shape[0])], axis=1)


def put(ref, rows, value):
    for tile in range(ref.shape[0]):
        ref[tile, rows, :] = value[:, tile * 128 : (tile + 1) * 128]


def rolled(x, shift):
    shift = shift % 128
    return x if shift == 0 else pltpu.roll(x, shift, 1)


def kernel(
    n,
    wide,
    state_hbm,
    source_hbm,
    gain_hbm,
    basis_hbm,
    ahead_hbm,
    back_hbm,
    mix_ref,
    frequency_ref,
    phase_ref,
    owner_ref,
    slot_ref,
    cycle_ref,
    relaxed_hbm,
    residual_hbm,
    stage,
    stage_source,
    gain,
    basis,
    ahead,
    back,
    s0,
    s1,
    source,
    res,
    basis_hi,
    basis_lo,
    turned_hi,
    turned_lo,
    gain_rows,
    strips0,
    strips1,
    inflow,
    modes_out,
    modes_in,
    late_out,
    late_in,
    first_out,
    first_in,
    second_out,
    second_in,
    packed,
    ghosts,
    load_sem,
    a2a_send,
    a2a_recv,
    strip_send,
    strip_recv,
    halo_send,
    halo_recv,
):
    azi = MODES * n
    quarter = azi // 4
    rad = RD * n
    nz = n // wide
    me = lax.axis_index("dom")
    my_z, my_w = me // wide, me % wide
    barrier = pltpu.get_barrier_semaphore()

    def load(i, src, dst):
        return pltpu.make_async_copy(src, dst, load_sem.at[i])

    loads = [
        load(0, state_hbm, stage),
        load(1, ahead_hbm, ahead),
        load(2, source_hbm, stage_source),
        load(3, basis_hbm, basis),
        load(4, gain_hbm, gain),
        load(5, back_hbm, back),
    ]
    for copy in loads:
        copy.start()

    def greet(s, carry):
        pl.semaphore_signal(
            barrier, inc=1, device_id={"dom": (me + s) % n}, device_id_type=MESH
        )
        return carry

    lax.fori_loop(1, n, greet, 0)

    lane = lax.broadcasted_iota(jnp.int32, (1, 128), 1)
    row8 = lax.broadcasted_iota(jnp.int32, (8, 128), 0)
    lane8 = lax.broadcasted_iota(jnp.int32, (8, 128), 1)

    def exchange(i, out, into):
        def send(s, carry):
            peer = (me + s) % n
            pltpu.make_async_remote_copy(
                src_ref=out.at[pl.ds(pl.multiple_of(peer * 8, 8), 8)],
                dst_ref=into.at[pl.ds(pl.multiple_of(me * 8, 8), 8)],
                send_sem=a2a_send.at[i],
                recv_sem=a2a_recv.at[i],
                device_id={"dom": peer},
                device_id_type=MESH,
            ).start()
            return carry

        lax.fori_loop(1, n, send, 0)
        mine = pl.ds(pl.multiple_of(me * 8, 8), 8)
        into[mine, :] = out[mine, :]

    def arrived(sem, ref):
        pltpu.make_async_copy(ref, ref, sem).wait()

    def exchange_wait(i, into):
        arrived(a2a_recv.at[i], into.at[pl.ds(0, (n - 1) * 8)])

    def strip_z(i, strips):
        mine = pl.ds(pl.multiple_of((my_w * nz + my_z) * 8, 8), 8)

        def send(s, carry):
            peer = (my_z + s) % nz * wide + my_w
            pltpu.make_async_remote_copy(
                src_ref=strips.at[mine],
                dst_ref=strips.at[mine],
                send_sem=strip_send.at[2 * i],
                recv_sem=strip_recv.at[2 * i],
                device_id={"dom": peer},
                device_id_type=MESH,
            ).start()
            return carry

        lax.fori_loop(1, nz, send, 0)

    def strip_w(i, strips):
        arrived(strip_recv.at[2 * i], strips.at[pl.ds(0, (nz - 1) * 8)])
        mine = pl.ds(pl.multiple_of(my_w * nz * 8, 8), nz * 8)

        def send(s, carry):
            peer = my_z * wide + (my_w + s) % wide
            pltpu.make_async_remote_copy(
                src_ref=strips.at[mine],
                dst_ref=strips.at[mine],
                send_sem=strip_send.at[2 * i + 1],
                recv_sem=strip_recv.at[2 * i + 1],
                device_id={"dom": peer},
                device_id_type=MESH,
            ).start()
            return carry

        lax.fori_loop(1, wide, send, 0)

    def strip_wait(i, strips):
        arrived(strip_recv.at[2 * i + 1], strips.at[pl.ds(0, (wide - 1) * nz * 8)])

    def halo_copies(i, low_src, low_dst, up_src, up_dst):
        down = pltpu.make_async_remote_copy(
            src_ref=low_src,
            dst_ref=up_dst,
            send_sem=halo_send.at[2 * i],
            recv_sem=halo_recv.at[2 * i],
            device_id={"dom": jnp.maximum(me - 1, 0)},
            device_id_type=MESH,
        )
        up = pltpu.make_async_remote_copy(
            src_ref=up_src,
            dst_ref=low_dst,
            send_sem=halo_send.at[2 * i + 1],
            recv_sem=halo_recv.at[2 * i + 1],
            device_id={"dom": jnp.minimum(me + 1, n - 1)},
            device_id_type=MESH,
        )
        return down, up

    def halo_start(copies):
        @pl.when(me > 0)
        def _():
            copies[0].start()

        @pl.when(me < n - 1)
        def _():
            copies[1].start()

    def halo_recv_wait(copies):
        @pl.when(me < n - 1)
        def _():
            copies[0].wait_recv()

        @pl.when(me > 0)
        def _():
            copies[1].wait_recv()

    def halo_send_wait(copies):
        @pl.when(me > 0)
        def _():
            copies[0].wait_send()

        @pl.when(me < n - 1)
        def _():
            copies[1].wait_send()

    def line_halo(i, s):
        return halo_copies(
            i,
            s.at[:, pl.ds(OWN, LINE)],
            s.at[:, pl.ds(0, LINE)],
            s.at[:, pl.ds(OWN + 3 * LINE, LINE)],
            s.at[:, pl.ds(UPPER, LINE)],
        )

    def spread(staged, dst, first):
        def body(cf, carry):
            for a in range(AX):
                put(dst, pl.ds(first + cf * 8 + a, RD, stride=LINE), staged[cf, a])
            return carry

        lax.fori_loop(0, 10, body, 0)

    def collect(src, staged):
        def body(cf, carry):
            for a in range(AX):
                staged[cf, a] = get(src, pl.ds(cf * 8 + a, RD, stride=LINE))
            return carry

        lax.fori_loop(0, 10, body, 0)

    def make_strip(s, strips):
        def body(r, acc):
            base = pl.multiple_of(OWN + r * LINE, 8)
            part = jnp.zeros((8, 128), F32)
            for cf in range(10):
                ends = jnp.where(
                    lane8 == 0,
                    s[0, pl.ds(base + cf * 8, 8), :],
                    s[s.shape[0] - 1, pl.ds(base + cf * 8, 8), :],
                )
                part = jnp.where(lane8 // 2 == cf * 4, rolled(ends, cf * 8 + 1), part)
            part = pltpu.roll(part, 2 * r, 1)
            return jnp.where(lane8 % 8 // 2 == r, part, acc)

        tile = lax.fori_loop(0, RD, body, jnp.zeros((8, 128), F32))
        mine = pl.ds(pl.multiple_of((my_w * nz + my_z) * 8, 8), 8)
        strips[mine, :] = tile

    angle = jnp.broadcast_to(phase_ref[0], (8, 128))
    cos_value, sin_value = jnp.cos(angle), jnp.sin(angle)

    def make_inflow(strips):
        def body(a, acc):
            for side in range(2):
                for r in range(RD):
                    face = side * AX * RD + a * RD + r
                    owner = owner_ref[face]
                    slot = slot_ref[face]
                    tile = owner % wide * nz + owner // wide
                    entry = strips[pl.ds(tile * 8 + slot // RD, 1), :]
                    shift = 2 * (r - slot % RD) + 1 - 2 * side + 128
                    moved = pltpu.roll(jnp.broadcast_to(entry, (8, 128)), shift, 1)
                    here = (row8 == a) & (lane8 % 8 == 2 * r + 1 - side)
                    acc = jnp.where(here, moved, acc)
            return acc

        partner = lax.fori_loop(0, AX, body, jnp.zeros((8, 128), F32))
        other = jnp.where(lane8 < 40, rolled(partner, -40), rolled(partner, 40))
        plus = (lane8 < 40) == (lane8 % 2 == 1)
        inflow[...] = cos_value * partner + jnp.where(plus, sin_value, -sin_value) * other

    def mixes(g, x):
        total = mix_ref[g, 0] * x[0]
        for f in range(1, 5):
            total = total + mix_ref[g, f] * x[f]
        return total

    frequency = frequency_ref[0]
    first_lane = lax.broadcasted_iota(jnp.int32, (8, azi), 1) == 0
    last_lane = lax.broadcasted_iota(jnp.int32, (8, azi), 1) == azi - 1
    row = lax.broadcasted_iota(jnp.int32, (8, azi), 0)

    def sweep(s, emit):
        def body(r, carry):
            base = pl.multiple_of(OWN + r * LINE, 8)
            above = pl.multiple_of(base + LINE + r // 3 * PAD, 8)
            here = pltpu.roll(inflow[...], 128 - 2 * r, 1)
            x = [get(s, pl.ds(base + cf * 8, 8)) for cf in range(10)]
            for c in range(2):
                for g in range(5):
                    cf = 5 * c + g
                    mine = x[cf]
                    other = x[5 * (1 - c) + g]
                    turn = frequency * other
                    center = 6.0 * mine + mixes(g, x[5 * c : 5 * c + 5])
                    center = center - turn if c == 0 else center + turn
                    along = jnp.where(row == 7, 0.0, pltpu.roll(mine, 7, 0)) + jnp.where(
                        row == 0, 0.0, pltpu.roll(mine, 1, 0)
                    )
                    lines = get(s, pl.ds(base - LINE + cf * 8, 8)) + get(
                        s, pl.ds(above + cf * 8, 8)
                    )
                    ends = rolled(here, -(cf * 8 + 1))
                    ends = jnp.concatenate([ends] * (azi // 128), axis=1)
                    after = jnp.where(last_lane, ends, pltpu.roll(mine, azi - 1, 1))
                    before = jnp.where(first_lane, ends, pltpu.roll(mine, 1, 1))
                    at = pl.multiple_of(r * LINE, 8) + cf * 8
                    image = center - (along + lines + (after + before))
                    emit(at, mine, get(source, pl.ds(at, 8)) - image)
            return carry

        lax.fori_loop(0, RD, body, 0)

    def forward(s, out):
        halves = []
        for c in range(2):
            blocks = [
                get(s, pl.ds(OWN + r * LINE + c * 40 + 7 * x, 8, stride=8))
                for r in range(RD)
                for x in range(2)
            ]
            halves.append(jnp.concatenate(blocks, axis=0))
        re, im = ([h[:, a * quarter : (a + 1) * quarter] for a in range(4)] for h in halves)
        se, de, so, do = re[0] + re[2], re[0] - re[2], re[1] + re[3], re[1] - re[3]
        te, ue, to, uo = im[0] + im[2], im[0] - im[2], im[1] + im[3], im[1] - im[3]
        classes = [(se + so, te + to), (de + uo, ue - do), (se - so, te - to), (de - uo, ue + do)]
        modes = [None] * MODES
        for b, (yr, yi) in enumerate(classes):
            y = jnp.concatenate(
                [jnp.concatenate([yr, yi], axis=0), jnp.concatenate([yi, -yr], axis=0)], axis=1
            )
            z = dot3((ahead[0, b], ahead[1, b]), split(y), ((1,), (1,)))
            modes[b], modes[4 + b] = z[:n], z[n:]
        for f in range(5):
            part = rolled(modes[0], -f)
            for j in range(1, MODES):
                part = jnp.where(lane % 8 == j, rolled(modes[j], j - f), part)
            out[pl.ds(f, n, stride=8), :] = part

    def cycle_weight(g, f):
        return jnp.where(lane // 8 % 2 == 0, cycle_ref[g * 5 + f], cycle_ref[25 + g * 5 + f])

    block = lane // 16 % 4

    def filtered(modes):
        blended = []
        for g in range(5):
            total = cycle_weight(g, 0) * modes[0]
            for f in range(1, 5):
                total = total + cycle_weight(g, f) * modes[f]
            blended.append(total)
        for r in range(RD):
            part = rolled(blended[0], -16 * r)
            for g in range(1, 4):
                part = jnp.where(block == g, rolled(blended[g], 16 * (g - r)), part)
            packed[0, pl.ds(r, n, stride=RD), :] = part
            packed[1, pl.ds(r, n, stride=RD), :] = rolled(blended[4], -16 * r)
        x = jnp.concatenate([packed[0], packed[1]], axis=1)
        radial = dot3((basis_hi[...], basis_lo[...]), split(x))
        radial = radial * gain_rows[...]
        back_r = dot3((turned_hi[...], turned_lo[...]), split(radial))
        packed[0] = back_r[:, :128]
        packed[1] = back_r[:, 128:]
        lines0 = [packed[0, pl.ds(r, n, stride=RD), :] for r in range(RD)]
        lines1 = [packed[1, pl.ds(r, n, stride=RD), :] for r in range(RD)]
        result = []
        for g in range(5):
            lines, place = (lines0, g) if g < 4 else (lines1, 0)
            part = rolled(lines[0], -16 * place)
            for r in range(1, RD):
                part = jnp.where(block == r, rolled(lines[r], 16 * (r - place)), part)
            result.append(part)
        return result

    def inverse(modes):
        spread_modes = [modes[pl.ds(g, n, stride=8), :] for g in range(5)]
        z = []
        for j in range(MODES):
            part = rolled(spread_modes[0], -j)
            for g in range(1, 5):
                part = jnp.where(lane % 8 == g, rolled(spread_modes[g], g - j), part)
            z.append(part)
        v = []
        for b in range(4):
            turned = jnp.concatenate([z[b], z[4 + b]], axis=0).T
            y = jnp.concatenate(
                [turned, jnp.concatenate([-turned[64:], turned[:64]], axis=0)], axis=1
            )
            v.append(dot3(split(y), (back[0, b], back[1, b])))
        s, d, p, q = v[0] + v[2], v[0] - v[2], v[1] + v[3], v[1] - v[3]
        iq = jnp.concatenate([-q[64:], q[:64]], axis=0)
        points = jnp.concatenate([s + p, d + iq, s - p, d - iq], axis=1)
        for c in range(2):
            for r in range(RD):
                put(
                    ghosts,
                    pl.ds(r * 32 + c * 16, 16),
                    points[c * 64 + r * 16 : c * 64 + r * 16 + 16],
                )

    def add_ghosts(dst, first, values, start, scale):
        for c in range(2):
            for x in range(2):
                rows = pl.ds(first + c * 40 + 7 * x, 5, stride=8)
                ghost = get(values, pl.ds(start + c * 16 + x * 8, 8))[:5]
                put(dst, rows, get(dst, rows) + scale * ghost)

    seventh = 1.0 / 7.0
    loads[0].wait()
    spread(stage, s0, OWN)
    for s in (s0, s1):
        put(s, pl.ds(OWN + RD * LINE, PAD), jnp.zeros((PAD, azi), F32))

    @pl.when(me == 0)
    def _():
        for s in (s0, s1):
            put(s, pl.ds(0, LINE), jnp.zeros((LINE, azi), F32))

    @pl.when(me == n - 1)
    def _():
        for s in (s0, s1):
            put(s, pl.ds(UPPER, LINE), jnp.zeros((LINE, azi), F32))

    make_strip(s0, strips0)
    pl.semaphore_wait(barrier, n - 1)
    strip_z(0, strips0)
    halo0 = line_halo(0, s0)
    halo_start(halo0)

    loads[1].wait()
    forward(s0, modes_out)
    strip_w(0, strips0)
    exchange(0, modes_out, modes_in)

    loads[2].wait()
    spread(stage_source, source, 0)
    loads[3].wait()
    whole = basis[...]
    basis_hi[...], basis_lo[...] = split(whole)
    turned_hi[...], turned_lo[...] = split(whole.T)
    loads[4].wait()
    rows0 = [gain[x, g] for c in range(2) for g in range(4) for x in range(2)]
    rows1 = [gain[x, 4] for c in range(2) for g in range(4) for x in range(2)]
    gain_rows[:, :128] = jnp.concatenate(rows0, axis=0).T
    gain_rows[:, 128:] = jnp.concatenate(rows1, axis=0).T
    loads[5].wait()

    strip_wait(0, strips0)
    make_inflow(strips0)
    halo_recv_wait(halo0)

    def emit_base(at, mine, value):
        put(s1, pl.ds(OWN + at, 8), mine + value * seventh)

    sweep(s0, emit_base)
    halo1 = line_halo(1, s1)
    forward(s1, late_out)
    exchange(1, late_out, late_in)

    exchange_wait(0, modes_in)
    first = filtered([modes_in[pl.ds(f, n, stride=8), :] for f in range(5)])
    for g in range(5):
        first_out[pl.ds(g, n, stride=8), :] = first[g]
    exchange(2, first_out, first_in)

    exchange_wait(1, late_in)
    second = filtered(
        [
            late_in[pl.ds(f, n, stride=8), :] + seventh * first_out[pl.ds(f, n, stride=8), :]
            for f in range(5)
        ]
    )
    for g in range(5):
        second_out[pl.ds(g, n, stride=8), :] = second[g]
    exchange(3, second_out, second_in)

    exchange_wait(2, first_in)
    inverse(first_in)

    def own_ghosts(r, carry):
        add_ghosts(s1, OWN + r * LINE, ghosts, r * 32, seventh)
        return carry

    lax.fori_loop(0, RD, own_ghosts, 0)
    make_strip(s1, strips1)
    strip_z(1, strips1)
    halo_start(halo1)
    strip_w(1, strips1)
    exchange_wait(3, second_in)
    inverse(second_in)
    halo_recv_wait(halo1)
    strip_wait(1, strips1)
    make_inflow(strips1)

    def emit_residual(at, mine, value):
        put(res, pl.ds(at, 8), value)

    sweep(s1, emit_residual)

    def last_ghosts(r, carry):
        add_ghosts(res, r * LINE, ghosts, r * 32, 1.0)
        return carry

    lax.fori_loop(0, RD, last_ghosts, 0)
    collect(res, stage_source)
    write_residual = pltpu.make_async_copy(stage_source, residual_hbm, load_sem.at[0])
    write_residual.start()

    def relax(i, carry):
        at = pl.multiple_of(i * 16, 8)
        rows = pl.ds(at, 16)
        put(res, rows, get(s1, pl.ds(OWN + at, 16)) + get(res, rows) * seventh)
        return carry

    lax.fori_loop(0, RD * LINE // 16, relax, 0)
    collect(res, stage)
    write_relaxed = pltpu.make_async_copy(stage, relaxed_hbm, load_sem.at[1])
    write_relaxed.start()

    for i, out in enumerate((modes_out, late_out, first_out, second_out)):
        arrived(a2a_send.at[i], out.at[pl.ds(0, (n - 1) * 8)])
    for i, strips in enumerate((strips0, strips1)):
        arrived(strip_send.at[2 * i], strips.at[pl.ds(0, (nz - 1) * 8)])
        arrived(strip_send.at[2 * i + 1], strips.at[pl.ds(0, (wide - 1) * nz * 8)])
    halo_send_wait(halo0)
    halo_send_wait(halo1)
    write_residual.wait()
    write_relaxed.wait()


def on_device(
    n,
    initial_state,
    source,
    field_coupling,
    frequency,
    phase_angle,
    face_owner,
    face_slot,
    radial_basis,
    cycle_coupling,
    cycle_gain,
):
    azi = MODES * n
    rad = RD * n
    quarter = azi // 4
    wide = 8 if n >= 64 else 4
    ahead, back = fourier_tables(n)
    shape = (10, AX, RD, azi)
    hbm = pl.BlockSpec(memory_space=pl.ANY)
    smem = pl.BlockSpec(memory_space=pltpu.SMEM)
    vmem = pltpu.VMEM
    peers = (n * 8, 128)
    return pl.pallas_call(
        functools.partial(kernel, n, wide),
        out_shape=(jax.ShapeDtypeStruct(shape, F32), jax.ShapeDtypeStruct(shape, F32)),
        in_specs=[hbm] * 6 + [smem] * 6,
        out_specs=(hbm, hbm),
        scratch_shapes=[
            vmem(shape, F32),
            vmem(shape, F32),
            vmem((2, 5, MODES, rad), F32),
            vmem((rad, rad), F32),
            vmem((2, 4, quarter, 2 * quarter), BF16),
            vmem((2, 4, 2 * quarter, quarter), BF16),
            vmem((azi // 128, ROWS, 128), F32),
            vmem((azi // 128, ROWS, 128), F32),
            vmem((azi // 128, RD * LINE, 128), F32),
            vmem((azi // 128, RD * LINE, 128), F32),
            vmem((rad, rad), BF16),
            vmem((rad, rad), BF16),
            vmem((rad, rad), BF16),
            vmem((rad, rad), BF16),
            vmem((rad, 256), F32),
            vmem(peers, F32),
            vmem(peers, F32),
            vmem((8, 128), F32),
            *[vmem(peers, F32) for _ in range(8)],
            vmem((2, rad, 128), F32),
            vmem((azi // 128, RD * 32, 128), F32),
            pltpu.SemaphoreType.DMA((6,)),
            pltpu.SemaphoreType.DMA((4,)),
            pltpu.SemaphoreType.DMA((4,)),
            pltpu.SemaphoreType.DMA((4,)),
            pltpu.SemaphoreType.DMA((4,)),
            pltpu.SemaphoreType.DMA((4,)),
            pltpu.SemaphoreType.DMA((4,)),
        ],
        compiler_params=pltpu.CompilerParams(
            collective_id=0, has_side_effects=True, vmem_limit_bytes=40 * 1024 * 1024
        ),
    )(
        initial_state,
        source,
        jnp.transpose(cycle_gain, (0, 1, 3, 2)),
        radial_basis,
        jnp.asarray(ahead),
        jnp.asarray(back),
        field_coupling,
        frequency,
        phase_angle,
        face_owner.reshape(-1),
        face_slot,
        cycle_coupling.reshape(-1),
    )


def solution(mesh):
    P = jax.sharding.PartitionSpec
    state = P("ibpa", None, "dom", None)
    in_specs = (
        state,
        state,
        P(),
        P(),
        P("ibpa"),
        P("dom", None),
        P("dom"),
        P(),
        P(),
        P(None, None, None, "dom"),
    )
    return jax.shard_map(
        functools.partial(on_device, mesh.shape["dom"]),
        mesh=mesh,
        in_specs=in_specs,
        out_specs=(state, state),
        check_vma=False,
    )
```

profile of v0, /device:TPU:1, one launch (start us, length us, event | category | flops | bytes accessed | tf_op | source)
XLA Modules:
  0.0 70.2 jit_solution(319528863230834550)
XLA Ops:
  0.6 0.0 copy-start.9
  1.9 0.0 copy-done.9
  2.0 0.0 copy-start.6
  2.0 0.0 copy-start.7
  2.0 0.0 copy-start.8
  2.0 0.1 reshape.11.cycle_ref
  2.1 0.6 copy-done.6
  2.7 0.0 copy-done.7
  2.7 0.0 copy-done.8
  2.7 0.0 copy-start
  2.7 1.1 %copy-done = f32[10,8,4,512]{3,2,1,0:T(4,128)S(1)} copy-done((f32[10,8,4,512]{3,2,1,0:T(4,128)S(1)}, f32[10,8,4,512]{3,2,1,0:T(4,128)}, u32[]{:S(2)}) %copy-start) | copy-done | bytes 655384
  3.7 0.0 copy-start.1
  3.8 1.1 %copy-done.1 = f32[10,8,4,512]{3,2,1,0:T(4,128)S(1)} copy-done((f32[10,8,4,512]{3,2,1,0:T(4,128)S(1)}, f32[10,8,4,512]{3,2,1,0:T(4,128)}, u32[]{:S(2)}) %copy-start.1) | copy-done | bytes 655384
  4.8 0.0 copy-start.2
  4.8 1.0 %copy-done.2 = bf16[2,4,256,128]{3,2,1,0:T(8,128)(2,1)S(1)} copy-done((bf16[2,4,256,128]{3,2,1,0:T(8,128)(2,1)S(1)}, bf16[2,4,256,128]{3,2,1,0:T(8,128)(2,1)}, u32[]{:S(2)}) %copy-start.2) | copy-done | bytes 524312
  5.9 0.0 copy-start.3
  5.9 1.0 %copy-done.3 = bf16[2,4,128,256]{3,2,1,0:T(8,128)(2,1)S(1)} copy-done((bf16[2,4,128,256]{3,2,1,0:T(8,128)(2,1)S(1)}, bf16[2,4,128,256]{3,2,1,0:T(8,128)(2,1)}, u32[]{:S(2)}) %copy-start.3) | copy-done | bytes 524312
  6.9 0.0 copy-start.4
  6.9 0.9 %copy-done.4 = f32[256,256]{1,0:T(8,128)S(1)} copy-done((f32[256,256]{1,0:T(8,128)S(1)}, f32[256,256]{1,0:T(8,128)}, u32[]{:S(2)}) %copy-start.4) | copy-done | bytes 262168
  7.9 0.0 copy-start.5
  7.9 0.9 %copy-done.5 = f32[2,5,256,8]{2,3,1,0:T(8,128)S(1)} copy-done((f32[2,5,256,8]{2,3,1,0:T(8,128)S(1)}, f32[2,5,256,8]{2,3,1,0:T(8,128)}, u32[]{:S(2)}) %copy-start.5) | copy-done | bytes 81944
  8.8 59.8 %shard_map.131 = (f32[10,8,4,512]{3,2,1,0:T(4,128)S(1)}, f32[10,8,4,512]{3,2,1,0:T(4,128)S(1)}) custom-call(f32[10,8,4,512]{3,2,1,0:T(4,128)S(1)} %copy-done, f32[10,8,4,512]{3,2,1,0:T(4,128)S(1)} %copy-done.1, f32[2,5,8,256]{3,2,1,0:T(8,128)S(1)} %bitcast.2, f32[256,256]{1,0:T(8,128)S(1)} %copy-done.4, bf16[2,4,128,256]{3,2,1,0:T(8,128)(2,1)S(1)} %copy-done.3, ...), custom_call_target="tpu_custom_call" | custom-call | tf_op jit(solution)/shard_map/pallas_call | solution.py:616
  68.6 0.8 %copy.20 = f32[10,8,4,512]{3,2,1,0:T(4,128)} copy(f32[10,8,4,512]{3,2,1,0:T(4,128)S(1)} %get-tuple-element.4) | data formatting | bytes 1310720
  69.4 0.8 %copy.21 = f32[10,8,4,512]{3,2,1,0:T(4,128)} copy(f32[10,8,4,512]{3,2,1,0:T(4,128)S(1)} %get-tuple-element.5) | data formatting | bytes 1310720
  (1 shorter events, 0.0 us)
Async XLA Ops:
  0.6 1.3 %copy-start.9 = (f32[2,5,5]{2,0,1:T(2,128)S(1)}, f32[2,5,5]{2,0,1:T(2,128)}, u32[]{:S(2)}) copy-start(f32[2,5,5]{2,0,1:T(2,128)} %param.20) | copy-start | bytes 604
  2.0 0.7 copy-start.6
  2.0 0.7 copy-start.7
  2.0 0.7 copy-start.8
  2.7 1.1 %copy-start = (f32[10,8,4,512]{3,2,1,0:T(4,128)S(1)}, f32[10,8,4,512]{3,2,1,0:T(4,128)}, u32[]{:S(2)}) copy-start(f32[10,8,4,512]{3,2,1,0:T(4,128)} %state_hbm.1) | copy-start | bytes 1966084
  3.7 1.1 %copy-start.1 = (f32[10,8,4,512]{3,2,1,0:T(4,128)S(1)}, f32[10,8,4,512]{3,2,1,0:T(4,128)}, u32[]{:S(2)}) copy-start(f32[10,8,4,512]{3,2,1,0:T(4,128)} %source_hbm.1) | copy-start | bytes 1966084
  4.8 1.0 %copy-start.2 = (bf16[2,4,256,128]{3,2,1,0:T(8,128)(2,1)S(1)}, bf16[2,4,256,128]{3,2,1,0:T(8,128)(2,1)}, u32[]{:S(2)}) copy-start(bf16[2,4,256,128]{3,2,1,0:T(8,128)(2,1)} %constant.5.clone.back_hbm) | copy-start | bytes 1572868
  5.9 1.0 %copy-start.3 = (bf16[2,4,128,256]{3,2,1,0:T(8,128)(2,1)S(1)}, bf16[2,4,128,256]{3,2,1,0:T(8,128)(2,1)}, u32[]{:S(2)}) copy-start(bf16[2,4,128,256]{3,2,1,0:T(8,128)(2,1)} %constant.4.clone.ahead_hbm) | copy-start | bytes 1572868
  6.9 0.9 %copy-start.4 = (f32[256,256]{1,0:T(8,128)S(1)}, f32[256,256]{1,0:T(8,128)}, u32[]{:S(2)}) copy-start(f32[256,256]{1,0:T(8,128)} %basis_hbm.1) | copy-start | bytes 786436
  7.9 0.9 %copy-start.5 = (f32[2,5,256,8]{2,3,1,0:T(8,128)S(1)}, f32[2,5,256,8]{2,3,1,0:T(8,128)}, u32[]{:S(2)}) copy-start(f32[2,5,256,8]{2,3,1,0:T(8,128)} %param.21) | copy-start | bytes 245764
where the time goes:
time: 70.7 us; the launch traced here: 70.2 us
  Pallas kernels  59.8 us (85%)
  local copies, waits for them, and re-layouts  8.44 us (12%)
  between operations  2 us (3%)
    pallas_call x1, Pallas kernels, on_device(): pl.pallas_call(functools.partial(kernel, n, wide), out_shape=(jax.ShapeDt...  59.8 us
    unnamed x23, local copies, waits for them, and re-layouts  8.36 us

commit v1 on v0

--- a/solution.py
+++ b/solution.py
@@ -105,7 +105,6 @@
     gain_rows,
     strips0,
     strips1,
-    inflow,
     modes_out,
     modes_in,
     late_out,
@@ -117,10 +116,10 @@
     packed,
     ghosts,
     load_sem,
-    a2a_send,
-    a2a_recv,
-    strip_send,
-    strip_recv,
+    all_send,
+    all_recv,
+    group_sent,
+    group_recv,
     halo_send,
     halo_recv,
 ):
@@ -132,6 +131,21 @@
     my_z, my_w = me // wide, me % wide
     barrier = pltpu.get_barrier_semaphore()
 
+    lane = lax.broadcasted_iota(jnp.int32, (1, 128), 1)
+    row8 = lax.broadcasted_iota(jnp.int32, (8, 128), 0)
+    lane8 = lax.broadcasted_iota(jnp.int32, (8, 128), 1)
+
+    def peer_of(i):
+        return (me + n // 2 + (i % 2) * ((i + 1) // 2) - (1 - i % 2) * (i // 2)) % n
+
+    def greet(step, carry):
+        pl.semaphore_signal(
+            barrier, inc=1, device_id={"dom": peer_of(step)}, device_id_type=MESH
+        )
+        return carry
+
+    lax.fori_loop(0, n - 1, greet, 0)
+
     def load(i, src, dst):
         return pltpu.make_async_copy(src, dst, load_sem.at[i])
 
@@ -146,78 +160,61 @@
     for copy in loads:
         copy.start()
 
-    def greet(s, carry):
-        pl.semaphore_signal(
-            barrier, inc=1, device_id={"dom": (me + s) % n}, device_id_type=MESH
-        )
-        return carry
-
-    lax.fori_loop(1, n, greet, 0)
-
-    lane = lax.broadcasted_iota(jnp.int32, (1, 128), 1)
-    row8 = lax.broadcasted_iota(jnp.int32, (8, 128), 0)
-    lane8 = lax.broadcasted_iota(jnp.int32, (8, 128), 1)
-
-    def exchange(i, out, into):
-        def send(s, carry):
-            peer = (me + s) % n
+    def send_all(i, src_of, dst):
+        def send(step, carry):
+            peer = peer_of(step)
             pltpu.make_async_remote_copy(
-                src_ref=out.at[pl.ds(pl.multiple_of(peer * 8, 8), 8)],
-                dst_ref=into.at[pl.ds(pl.multiple_of(me * 8, 8), 8)],
-                send_sem=a2a_send.at[i],
-                recv_sem=a2a_recv.at[i],
+                src_ref=src_of(peer),
+                dst_ref=dst,
+                send_sem=all_send.at[i],
+                recv_sem=all_recv.at[i],
                 device_id={"dom": peer},
                 device_id_type=MESH,
             ).start()
             return carry
 
-        lax.fori_loop(1, n, send, 0)
-        mine = pl.ds(pl.multiple_of(me * 8, 8), 8)
-        into[mine, :] = out[mine, :]
+        lax.fori_loop(0, n - 1, send, 0)
+
+    def tile_rows(device, count):
+        return pl.ds(pl.multiple_of(device * 8, 8), count)
+
+    def exchange(i, out, into):
+        send_all(i, lambda peer: out.at[tile_rows(peer, 5)], into.at[tile_rows(me, 5)])
+        into[tile_rows(me, 8), :] = out[tile_rows(me, 8), :]
 
     def arrived(sem, ref):
         pltpu.make_async_copy(ref, ref, sem).wait()
 
     def exchange_wait(i, into):
-        arrived(a2a_recv.at[i], into.at[pl.ds(0, (n - 1) * 8)])
-
-    def strip_z(i, strips):
-        mine = pl.ds(pl.multiple_of((my_w * nz + my_z) * 8, 8), 8)
-
-        def send(s, carry):
-            peer = (my_z + s) % nz * wide + my_w
+        arrived(all_recv.at[i], into.at[pl.ds(0, (n - 1) * 5)])
+
+    def group_send(i, count, peer_at, block):
+        def send(step, carry):
             pltpu.make_async_remote_copy(
-                src_ref=strips.at[mine],
-                dst_ref=strips.at[mine],
-                send_sem=strip_send.at[2 * i],
-                recv_sem=strip_recv.at[2 * i],
-                device_id={"dom": peer},
+                src_ref=block,
+                dst_ref=block,
+                send_sem=group_sent.at[i],
+                recv_sem=group_recv.at[i],
+                device_id={"dom": peer_at(step)},
                 device_id_type=MESH,
             ).start()
             return carry
 
-        lax.fori_loop(1, nz, send, 0)
+        lax.fori_loop(1, count, send, 0)
+
+    my_tile = my_w * nz + my_z
+
+    def strip_z(i, strips):
+        block = strips.at[tile_rows(my_tile, 8)]
+        group_send(2 * i, nz, lambda step: (my_z + step) % nz * wide + my_w, block)
 
     def strip_w(i, strips):
-        arrived(strip_recv.at[2 * i], strips.at[pl.ds(0, (nz - 1) * 8)])
-        mine = pl.ds(pl.multiple_of(my_w * nz * 8, 8), nz * 8)
-
-        def send(s, carry):
-            peer = my_z * wide + (my_w + s) % wide
-            pltpu.make_async_remote_copy(
-                src_ref=strips.at[mine],
-                dst_ref=strips.at[mine],
-                send_sem=strip_send.at[2 * i + 1],
-                recv_sem=strip_recv.at[2 * i + 1],
-                device_id={"dom": peer},
-                device_id_type=MESH,
-            ).start()
-            return carry
-
-        lax.fori_loop(1, wide, send, 0)
+        arrived(group_recv.at[2 * i], strips.at[pl.ds(0, (nz - 1) * 8)])
+        block = strips.at[tile_rows(my_w * nz, nz * 8)]
+        group_send(2 * i + 1, wide, lambda step: my_z * wide + (my_w + step) % wide, block)
 
     def strip_wait(i, strips):
-        arrived(strip_recv.at[2 * i + 1], strips.at[pl.ds(0, (wide - 1) * nz * 8)])
+        arrived(group_recv.at[2 * i + 1], strips.at[pl.ds(0, (wide - 1) * nz * 8)])
 
     def halo_copies(i, low_src, low_dst, up_src, up_dst):
         down = pltpu.make_async_remote_copy(
@@ -282,9 +279,9 @@
 
         lax.fori_loop(0, 10, body, 0)
 
-    def collect(src, staged):
+    def collect(src, staged, stations):
         def body(cf, carry):
-            for a in range(AX):
+            for a in stations:
                 staged[cf, a] = get(src, pl.ds(cf * 8 + a, RD, stride=LINE))
             return carry
 
@@ -304,9 +301,8 @@
             part = pltpu.roll(part, 2 * r, 1)
             return jnp.where(lane8 % 8 // 2 == r, part, acc)
 
-        tile = lax.fori_loop(0, RD, body, jnp.zeros((8, 128), F32))
-        mine = pl.ds(pl.multiple_of((my_w * nz + my_z) * 8, 8), 8)
-        strips[mine, :] = tile
+        tile = lax.fori_loop(0, RD, body, jnp.zeros((8, 128), F32), unroll=True)
+        strips[tile_rows(my_tile, 8), :] = tile
 
     angle = jnp.broadcast_to(phase_ref[0], (8, 128))
     cos_value, sin_value = jnp.cos(angle), jnp.sin(angle)
@@ -326,10 +322,10 @@
                     acc = jnp.where(here, moved, acc)
             return acc
 
-        partner = lax.fori_loop(0, AX, body, jnp.zeros((8, 128), F32))
+        partner = lax.fori_loop(0, AX, body, jnp.zeros((8, 128), F32), unroll=True)
         other = jnp.where(lane8 < 40, rolled(partner, -40), rolled(partner, 40))
         plus = (lane8 < 40) == (lane8 % 2 == 1)
-        inflow[...] = cos_value * partner + jnp.where(plus, sin_value, -sin_value) * other
+        return cos_value * partner + jnp.where(plus, sin_value, -sin_value) * other
 
     def mixes(g, x):
         total = mix_ref[g, 0] * x[0]
@@ -346,7 +342,6 @@
         def body(r, carry):
             base = pl.multiple_of(OWN + r * LINE, 8)
             above = pl.multiple_of(base + LINE + r // 3 * PAD, 8)
-            here = pltpu.roll(inflow[...], 128 - 2 * r, 1)
             x = [get(s, pl.ds(base + cf * 8, 8)) for cf in range(10)]
             for c in range(2):
                 for g in range(5):
@@ -362,16 +357,29 @@
                     lines = get(s, pl.ds(base - LINE + cf * 8, 8)) + get(
                         s, pl.ds(above + cf * 8, 8)
                     )
-                    ends = rolled(here, -(cf * 8 + 1))
-                    ends = jnp.concatenate([ends] * (azi // 128), axis=1)
-                    after = jnp.where(last_lane, ends, pltpu.roll(mine, azi - 1, 1))
-                    before = jnp.where(first_lane, ends, pltpu.roll(mine, 1, 1))
+                    after = jnp.where(last_lane, 0.0, pltpu.roll(mine, azi - 1, 1))
+                    before = jnp.where(first_lane, 0.0, pltpu.roll(mine, 1, 1))
                     at = pl.multiple_of(r * LINE, 8) + cf * 8
                     image = center - (along + lines + (after + before))
                     emit(at, mine, get(source, pl.ds(at, 8)) - image)
             return carry
 
         lax.fori_loop(0, RD, body, 0)
+
+    def add_inflow(strips, dst, first, scale):
+        flow = scale * make_inflow(strips)
+        last = dst.shape[0] - 1
+
+        def body(r, carry):
+            here = pltpu.roll(flow, 127 - 2 * r, 1)
+            for cf in range(10):
+                rows = pl.ds(pl.multiple_of(first + r * LINE, 8) + cf * 8, 8)
+                ends = rolled(here, -cf * 8)
+                dst[0, rows, :] = dst[0, rows, :] + jnp.where(lane8 == 0, ends, 0.0)
+                dst[last, rows, :] = dst[last, rows, :] + jnp.where(lane8 == 127, ends, 0.0)
+            return carry
+
+        lax.fori_loop(0, RD, body, 0, unroll=True)
 
     def forward(s, out):
         halves = []
@@ -484,16 +492,8 @@
             put(s, pl.ds(UPPER, LINE), jnp.zeros((LINE, azi), F32))
 
     make_strip(s0, strips0)
-    pl.semaphore_wait(barrier, n - 1)
-    strip_z(0, strips0)
-    halo0 = line_halo(0, s0)
-    halo_start(halo0)
-
     loads[1].wait()
     forward(s0, modes_out)
-    strip_w(0, strips0)
-    exchange(0, modes_out, modes_in)
-
     loads[2].wait()
     spread(stage_source, source, 0)
     loads[3].wait()
@@ -507,23 +507,42 @@
     gain_rows[:, 128:] = jnp.concatenate(rows1, axis=0).T
     loads[5].wait()
 
-    strip_wait(0, strips0)
-    make_inflow(strips0)
-    halo_recv_wait(halo0)
+    pl.semaphore_wait(barrier, n - 1)
+    strip_z(0, strips0)
+    halo0 = line_halo(0, s0)
+    halo_start(halo0)
+    exchange(0, modes_out, modes_in)
+    strip_w(0, strips0)
 
     def emit_base(at, mine, value):
         put(s1, pl.ds(OWN + at, 8), mine + value * seventh)
 
+    halo_recv_wait(halo0)
     sweep(s0, emit_base)
-    halo1 = line_halo(1, s1)
-    forward(s1, late_out)
-    exchange(1, late_out, late_in)
 
     exchange_wait(0, modes_in)
     first = filtered([modes_in[pl.ds(f, n, stride=8), :] for f in range(5)])
     for g in range(5):
         first_out[pl.ds(g, n, stride=8), :] = first[g]
     exchange(2, first_out, first_in)
+
+    strip_wait(0, strips0)
+    add_inflow(strips0, s1, OWN, seventh)
+    forward(s1, late_out)
+    exchange(1, late_out, late_in)
+
+    exchange_wait(2, first_in)
+    inverse(first_in)
+
+    def own_ghosts(r, carry):
+        add_ghosts(s1, OWN + r * LINE, ghosts, r * 32, seventh)
+        return carry
+
+    lax.fori_loop(0, RD, own_ghosts, 0, unroll=True)
+    make_strip(s1, strips1)
+    strip_z(1, strips1)
+    halo1 = line_halo(1, s1)
+    halo_start(halo1)
 
     exchange_wait(1, late_in)
     second = filtered(
@@ -535,59 +554,62 @@
     for g in range(5):
         second_out[pl.ds(g, n, stride=8), :] = second[g]
     exchange(3, second_out, second_in)
-
-    exchange_wait(2, first_in)
-    inverse(first_in)
-
-    def own_ghosts(r, carry):
-        add_ghosts(s1, OWN + r * LINE, ghosts, r * 32, seventh)
-        return carry
-
-    lax.fori_loop(0, RD, own_ghosts, 0)
-    make_strip(s1, strips1)
-    strip_z(1, strips1)
-    halo_start(halo1)
     strip_w(1, strips1)
-    exchange_wait(3, second_in)
-    inverse(second_in)
-    halo_recv_wait(halo1)
-    strip_wait(1, strips1)
-    make_inflow(strips1)
 
     def emit_residual(at, mine, value):
         put(res, pl.ds(at, 8), value)
 
+    halo_recv_wait(halo1)
     sweep(s1, emit_residual)
-
-    def last_ghosts(r, carry):
-        add_ghosts(res, r * LINE, ghosts, r * 32, 1.0)
-        return carry
-
-    lax.fori_loop(0, RD, last_ghosts, 0)
-    collect(res, stage_source)
-    write_residual = pltpu.make_async_copy(stage_source, residual_hbm, load_sem.at[0])
-    write_residual.start()
+    strip_wait(1, strips1)
+    add_inflow(strips1, res, 0, 1.0)
 
     def relax(i, carry):
         at = pl.multiple_of(i * 16, 8)
         rows = pl.ds(at, 16)
-        put(res, rows, get(s1, pl.ds(OWN + at, 16)) + get(res, rows) * seventh)
+        put(source, rows, get(s1, pl.ds(OWN + at, 16)) + get(res, rows) * seventh)
         return carry
 
-    lax.fori_loop(0, RD * LINE // 16, relax, 0)
-    collect(res, stage)
-    write_relaxed = pltpu.make_async_copy(stage, relaxed_hbm, load_sem.at[1])
-    write_relaxed.start()
+    lax.fori_loop(0, RD * LINE // 16, relax, 0, unroll=4)
+    writes = []
+
+    def write(i, staged, out, first_station, count):
+        part = (slice(None), pl.ds(first_station, count))
+        copy = pltpu.make_async_copy(staged.at[part], out.at[part], load_sem.at[i])
+        copy.start()
+        writes.append(copy)
+
+    middle = range(1, AX - 1)
+    collect(res, stage_source, middle)
+    write(0, stage_source, residual_hbm, 1, AX - 2)
+    collect(source, stage, middle)
+    write(1, stage, relaxed_hbm, 1, AX - 2)
+
+    exchange_wait(3, second_in)
+    inverse(second_in)
+
+    def last_ghosts(r, carry):
+        add_ghosts(res, r * LINE, ghosts, r * 32, 1.0)
+        add_ghosts(source, r * LINE, ghosts, r * 32, seventh)
+        return carry
+
+    lax.fori_loop(0, RD, last_ghosts, 0, unroll=True)
+    ends = (0, AX - 1)
+    collect(res, stage_source, ends)
+    collect(source, stage, ends)
+    for place, station in enumerate(ends):
+        write(2 + place, stage_source, residual_hbm, station, 1)
+        write(4 + place, stage, relaxed_hbm, station, 1)
 
     for i, out in enumerate((modes_out, late_out, first_out, second_out)):
-        arrived(a2a_send.at[i], out.at[pl.ds(0, (n - 1) * 8)])
+        arrived(all_send.at[i], out.at[pl.ds(0, (n - 1) * 5)])
     for i, strips in enumerate((strips0, strips1)):
-        arrived(strip_send.at[2 * i], strips.at[pl.ds(0, (nz - 1) * 8)])
-        arrived(strip_send.at[2 * i + 1], strips.at[pl.ds(0, (wide - 1) * nz * 8)])
+        arrived(group_sent.at[2 * i], strips.at[pl.ds(0, (nz - 1) * 8)])
+        arrived(group_sent.at[2 * i + 1], strips.at[pl.ds(0, (wide - 1) * nz * 8)])
     halo_send_wait(halo0)
     halo_send_wait(halo1)
-    write_residual.wait()
-    write_relaxed.wait()
+    for copy in writes:
+        copy.wait()
 
 
 def on_device(
@@ -606,7 +628,6 @@
     azi = MODES * n
     rad = RD * n
     quarter = azi // 4
-    wide = 8 if n >= 64 else 4
     ahead, back = fourier_tables(n)
     shape = (10, AX, RD, azi)
     hbm = pl.BlockSpec(memory_space=pl.ANY)
@@ -614,7 +635,7 @@
     vmem = pltpu.VMEM
     peers = (n * 8, 128)
     return pl.pallas_call(
-        functools.partial(kernel, n, wide),
+        functools.partial(kernel, n, 8 if n >= 64 else 4),
         out_shape=(jax.ShapeDtypeStruct(shape, F32), jax.ShapeDtypeStruct(shape, F32)),
         in_specs=[hbm] * 6 + [smem] * 6,
         out_specs=(hbm, hbm),
@@ -636,7 +657,6 @@
             vmem((rad, 256), F32),
             vmem(peers, F32),
             vmem(peers, F32),
-            vmem((8, 128), F32),
             *[vmem(peers, F32) for _ in range(8)],
             vmem((2, rad, 128), F32),
             vmem((azi // 128, RD * 32, 128), F32),
@@ -649,7 +669,7 @@
             pltpu.SemaphoreType.DMA((4,)),
         ],
         compiler_params=pltpu.CompilerParams(
-            collective_id=0, has_side_effects=True, vmem_limit_bytes=40 * 1024 * 1024
+            collective_id=0, has_side_effects=True, vmem_limit_bytes=62 * 1024 * 1024
         ),
     )(
         initial_state,

time: 70.7 us -> 55.8 us (0.79)
  Pallas kernels: 59.8 us -> 50.1 us
  local copies, waits for them, and re-layouts: 8.44 us -> 3.48 us
    pallas_call x1, Pallas kernels: 59.8 us -> 50.1 us  [on_device(): pl.pallas_call(functools.partial(kernel, n, 8 if n >= 64 else 4), out_sha...]
    unnamed x23 -> x7, local copies, waits for them, and re-layouts: 8.36 us -> 2.88 us
where the time goes in v1:
time: 55.8 us; the launch traced here: 55.6 us
  Pallas kernels  50.1 us (90%)
  local copies, waits for them, and re-layouts  3.48 us (6%)
  between operations  1.98 us (4%)
    pallas_call x1, Pallas kernels, on_device(): pl.pallas_call(functools.partial(kernel, n, 8 if n >= 64 else 4), out_sha...  50.1 us
    unnamed x7, local copies, waits for them, and re-layouts  2.88 us

profile of v1, /device:TPU:1, one launch (start us, length us, event | category | flops | bytes accessed | tf_op | source)
XLA Modules:
  0.0 55.6 jit_solution(4424530782618479114)
XLA Ops:
  0.6 0.0 copy-start.1
  1.9 0.0 copy-done.1
  2.0 0.6 %reshape.11.cycle_ref = f32[50]{0:T(128)} reshape(f32[2,5,5]{2,1,0:T(8,128)S(1)} %copy.15) | data formatting | bytes 400 | tf_op jit(solution)/shard_map/reshape | solution.py:686
  2.6 50.1 %shard_map.131 = (f32[10,8,4,512]{3,2,1,0:T(4,128)}, f32[10,8,4,512]{3,2,1,0:T(4,128)}) custom-call(f32[10,8,4,512]{3,2,1,0:T(4,128)} %state_hbm.1, f32[10,8,4,512]{3,2,1,0:T(4,128)} %source_hbm.1, f32[2,5,8,256]{3,2,1,0:T(8,128)} %bitcast.2, f32[256,256]{1,0:T(8,128)} %basis_hbm.1, bf16[2,4,128,256]{3,2,1,0:T(8,128)(2,1)} %constant.4.clone.ahead_hbm, ...), custom_call_target="tpu_custom_call" | custom-call | tf_op jit(solution)/shard_map/pallas_call | solution.py:637
  52.7 0.0 copy-start
  52.7 2.0 %copy.20 = f32[10,8,4,512]{3,2,1,0:T(4,128)} copy(f32[10,8,4,512]{3,2,1,0:T(4,128)} %get-tuple-element.4) | data formatting | bytes 1310720
  54.8 0.0 copy-done
  54.8 0.8 %copy.21 = f32[10,8,4,512]{3,2,1,0:T(4,128)} copy(f32[10,8,4,512]{3,2,1,0:T(4,128)S(1)} %copy-done) | data formatting | bytes 1310720
  (1 shorter events, 0.0 us)
Async XLA Ops:
  0.6 1.3 %copy-start.1 = (f32[2,5,5]{2,0,1:T(2,128)S(1)}, f32[2,5,5]{2,0,1:T(2,128)}, u32[]{:S(2)}) copy-start(f32[2,5,5]{2,0,1:T(2,128)} %param.20) | copy-start | bytes 604
  52.7 2.0 %copy-start = (f32[10,8,4,512]{3,2,1,0:T(4,128)S(1)}, f32[10,8,4,512]{3,2,1,0:T(4,128)}, u32[]{:S(2)}) copy-start(f32[10,8,4,512]{3,2,1,0:T(4,128)} %get-tuple-element.5) | copy-start | bytes 1966084

commit v2 on v1

--- a/solution.py
+++ b/solution.py
@@ -86,8 +86,8 @@
     owner_ref,
     slot_ref,
     cycle_ref,
-    relaxed_hbm,
-    residual_hbm,
+    relaxed,
+    residual,
     stage,
     stage_source,
     gain,
@@ -173,7 +173,7 @@
             ).start()
             return carry
 
-        lax.fori_loop(0, n - 1, send, 0)
+        lax.fori_loop(0, n - 1, send, 0, unroll=True)
 
     def tile_rows(device, count):
         return pl.ds(pl.multiple_of(device * 8, 8), count)
@@ -200,21 +200,21 @@
             ).start()
             return carry
 
-        lax.fori_loop(1, count, send, 0)
+        lax.fori_loop(1, count, send, 0, unroll=True)
 
     my_tile = my_w * nz + my_z
 
     def strip_z(i, strips):
-        block = strips.at[tile_rows(my_tile, 8)]
+        block = strips.at[pl.ds(my_tile, 1), pl.ds(0, 5)]
         group_send(2 * i, nz, lambda step: (my_z + step) % nz * wide + my_w, block)
 
     def strip_w(i, strips):
-        arrived(group_recv.at[2 * i], strips.at[pl.ds(0, (nz - 1) * 8)])
-        block = strips.at[tile_rows(my_w * nz, nz * 8)]
+        arrived(group_recv.at[2 * i], strips.at[pl.ds(0, nz - 1), pl.ds(0, 5)])
+        block = strips.at[pl.ds(my_w * nz, nz), pl.ds(0, 5)]
         group_send(2 * i + 1, wide, lambda step: my_z * wide + (my_w + step) % wide, block)
 
     def strip_wait(i, strips):
-        arrived(group_recv.at[2 * i + 1], strips.at[pl.ds(0, (wide - 1) * nz * 8)])
+        arrived(group_recv.at[2 * i + 1], strips.at[pl.ds(0, (wide - 1) * nz), pl.ds(0, 5)])
 
     def halo_copies(i, low_src, low_dst, up_src, up_dst):
         down = pltpu.make_async_remote_copy(
@@ -287,6 +287,15 @@
 
         lax.fori_loop(0, 10, body, 0)
 
+    group8 = lane8 // 8 % 8
+
+    def by_field(x):
+        turned = jnp.zeros((8, 128), F32)
+        for delta in range(-7, 8):
+            moved = x if delta == 0 else pltpu.roll(rolled(x, 8 * delta), -delta % 8, 0)
+            turned = jnp.where(group8 - row8 == delta, moved, turned)
+        return turned
+
     def make_strip(s, strips):
         def body(r, acc):
             base = pl.multiple_of(OWN + r * LINE, 8)
@@ -302,7 +311,7 @@
             return jnp.where(lane8 % 8 // 2 == r, part, acc)
 
         tile = lax.fori_loop(0, RD, body, jnp.zeros((8, 128), F32), unroll=True)
-        strips[tile_rows(my_tile, 8), :] = tile
+        strips[my_tile] = by_field(jnp.where(lane8 < 40, tile, rolled(tile, 24)))
 
     angle = jnp.broadcast_to(phase_ref[0], (8, 128))
     cos_value, sin_value = jnp.cos(angle), jnp.sin(angle)
@@ -314,18 +323,18 @@
                     face = side * AX * RD + a * RD + r
                     owner = owner_ref[face]
                     slot = slot_ref[face]
-                    tile = owner % wide * nz + owner // wide
-                    entry = strips[pl.ds(tile * 8 + slot // RD, 1), :]
-                    shift = 2 * (r - slot % RD) + 1 - 2 * side + 128
-                    moved = pltpu.roll(jnp.broadcast_to(entry, (8, 128)), shift, 1)
-                    here = (row8 == a) & (lane8 % 8 == 2 * r + 1 - side)
-                    acc = jnp.where(here, moved, acc)
+                    entry = strips[owner % wide * nz + owner // wide]
+                    to = a * 8 + 2 * r + 1 - side
+                    moved = pltpu.roll(entry, to - (slot * 2 + side) + 128, 1)
+                    acc = jnp.where(lane8 % 64 == to, moved, acc)
             return acc
 
         partner = lax.fori_loop(0, AX, body, jnp.zeros((8, 128), F32), unroll=True)
-        other = jnp.where(lane8 < 40, rolled(partner, -40), rolled(partner, 40))
-        plus = (lane8 < 40) == (lane8 % 2 == 1)
-        return cos_value * partner + jnp.where(plus, sin_value, -sin_value) * other
+        other = rolled(partner, 64)
+        plus = (lane8 < 64) == (lane8 % 2 == 1)
+        flow = cos_value * partner + jnp.where(plus, sin_value, -sin_value) * other
+        flow = by_field(flow)
+        return jnp.where(lane8 < 40, flow, rolled(flow, -24))
 
     def mixes(g, x):
         total = mix_ref[g, 0] * x[0]
@@ -408,7 +417,7 @@
             out[pl.ds(f, n, stride=8), :] = part
 
     def cycle_weight(g, f):
-        return jnp.where(lane // 8 % 2 == 0, cycle_ref[g * 5 + f], cycle_ref[25 + g * 5 + f])
+        return jnp.where(lane // 8 % 2 == 0, cycle_ref[g, 0, f], cycle_ref[g, 1, f])
 
     block = lane // 16 % 4
 
@@ -571,19 +580,9 @@
         return carry
 
     lax.fori_loop(0, RD * LINE // 16, relax, 0, unroll=4)
-    writes = []
-
-    def write(i, staged, out, first_station, count):
-        part = (slice(None), pl.ds(first_station, count))
-        copy = pltpu.make_async_copy(staged.at[part], out.at[part], load_sem.at[i])
-        copy.start()
-        writes.append(copy)
-
     middle = range(1, AX - 1)
-    collect(res, stage_source, middle)
-    write(0, stage_source, residual_hbm, 1, AX - 2)
-    collect(source, stage, middle)
-    write(1, stage, relaxed_hbm, 1, AX - 2)
+    collect(res, residual, middle)
+    collect(source, relaxed, middle)
 
     exchange_wait(3, second_in)
     inverse(second_in)
@@ -595,20 +594,26 @@
 
     lax.fori_loop(0, RD, last_ghosts, 0, unroll=True)
     ends = (0, AX - 1)
-    collect(res, stage_source, ends)
-    collect(source, stage, ends)
-    for place, station in enumerate(ends):
-        write(2 + place, stage_source, residual_hbm, station, 1)
-        write(4 + place, stage, relaxed_hbm, station, 1)
+    collect(res, residual, ends)
+    collect(source, relaxed, ends)
 
     for i, out in enumerate((modes_out, late_out, first_out, second_out)):
         arrived(all_send.at[i], out.at[pl.ds(0, (n - 1) * 5)])
     for i, strips in enumerate((strips0, strips1)):
-        arrived(group_sent.at[2 * i], strips.at[pl.ds(0, (nz - 1) * 8)])
-        arrived(group_sent.at[2 * i + 1], strips.at[pl.ds(0, (wide - 1) * nz * 8)])
+        arrived(group_sent.at[2 * i], strips.at[pl.ds(0, nz - 1), pl.ds(0, 5)])
+        arrived(group_sent.at[2 * i + 1], strips.at[pl.ds(0, (wide - 1) * nz), pl.ds(0, 5)])
     halo_send_wait(halo0)
     halo_send_wait(halo1)
-    for copy in writes:
+
+
+def write_kernel(relaxed, residual, relaxed_hbm, residual_hbm, sem):
+    copies = [
+        pltpu.make_async_copy(relaxed, relaxed_hbm, sem.at[0]),
+        pltpu.make_async_copy(residual, residual_hbm, sem.at[1]),
+    ]
+    for copy in copies:
+        copy.start()
+    for copy in copies:
         copy.wait()
 
 
@@ -634,11 +639,11 @@
     smem = pl.BlockSpec(memory_space=pltpu.SMEM)
     vmem = pltpu.VMEM
     peers = (n * 8, 128)
-    return pl.pallas_call(
+    relaxed, residual = pl.pallas_call(
         functools.partial(kernel, n, 8 if n >= 64 else 4),
-        out_shape=(jax.ShapeDtypeStruct(shape, F32), jax.ShapeDtypeStruct(shape, F32)),
+        out_shape=(vmem(shape, F32), vmem(shape, F32)),
         in_specs=[hbm] * 6 + [smem] * 6,
-        out_specs=(hbm, hbm),
+        out_specs=(pl.BlockSpec(memory_space=vmem), pl.BlockSpec(memory_space=vmem)),
         scratch_shapes=[
             vmem(shape, F32),
             vmem(shape, F32),
@@ -655,8 +660,8 @@
             vmem((rad, rad), BF16),
             vmem((rad, rad), BF16),
             vmem((rad, 256), F32),
-            vmem(peers, F32),
-            vmem(peers, F32),
+            vmem((n, 8, 128), F32),
+            vmem((n, 8, 128), F32),
             *[vmem(peers, F32) for _ in range(8)],
             vmem((2, rad, 128), F32),
             vmem((azi // 128, RD * 32, 128), F32),
@@ -683,8 +688,16 @@
         phase_angle,
         face_owner.reshape(-1),
         face_slot,
-        cycle_coupling.reshape(-1),
+        jnp.transpose(cycle_coupling, (1, 0, 2)),
     )
+    return pl.pallas_call(
+        write_kernel,
+        out_shape=(jax.ShapeDtypeStruct(shape, F32), jax.ShapeDtypeStruct(shape, F32)),
+        in_specs=[hbm, hbm],
+        out_specs=(hbm, hbm),
+        scratch_shapes=[pltpu.SemaphoreType.DMA((2,))],
+        compiler_params=pltpu.CompilerParams(vmem_limit_bytes=4 * 1024 * 1024),
+    )(relaxed, residual)
 
 
 def solution(mesh):

time: 55.8 us -> 50.3 us (0.901)
  local copies, waits for them, and re-layouts: 3.48 us -> 0 us
  Pallas kernels: 50.1 us -> 48.2 us
    pallas_call x1, Pallas kernels: 50.1 us -> 47.1 us  [on_device(): pl.pallas_call(functools.partial(kernel, n, 8 if n >= 64 else 4), out_sha...]
    unnamed x7 -> x0, local copies, waits for them, and re-layouts: 2.88 us -> none
    pallas_call x0 -> x1, Pallas kernels: none -> 1.07 us  [on_device(): pl.pallas_call(write_kernel, out_shape=(jax.ShapeDtypeStruct(shape, F32),...]
    reshape x1 -> x0, local copies, waits for them, and re-layouts: 0.59 us -> none  [on_device(): cycle_coupling.reshape(-1)]
where the time goes in v2:
time: 50.3 us; the launch traced here: 50.1 us
  Pallas kernels  48.2 us (96%)
  between operations  1.93 us (4%)
    pallas_call x1, Pallas kernels, on_device(): pl.pallas_call(functools.partial(kernel, n, 8 if n >= 64 else 4), out_sha...  47.1 us
    pallas_call x1, Pallas kernels, on_device(): pl.pallas_call(write_kernel, out_shape=(jax.ShapeDtypeStruct(shape, F32),...  1.07 us

profile of v2, /device:TPU:1, one launch (start us, length us, event | category | flops | bytes accessed | tf_op | source)
XLA Modules:
  0.0 50.1 jit_solution(14162512073161703109)
XLA Ops:
  1.9 47.1 %shard_map.131 = (f32[10,8,4,512]{3,2,1,0:T(4,128)S(1)}, f32[10,8,4,512]{3,2,1,0:T(4,128)S(1)}) custom-call(f32[10,8,4,512]{3,2,1,0:T(4,128)} %state_hbm.1, f32[10,8,4,512]{3,2,1,0:T(4,128)} %source_hbm.1, f32[2,5,8,256]{3,2,1,0:T(8,128)} %bitcast.3, f32[256,256]{1,0:T(8,128)} %basis_hbm.1, bf16[2,4,128,256]{3,2,1,0:T(8,128)(2,1)} %constant.4.clone.ahead_hbm, ...), custom_call_target="tpu_custom_call" | custom-call | tf_op jit(solution)/shard_map/pallas_call | solution.py:642
  49.0 1.1 %shard_map.132 = (f32[10,8,4,512]{3,2,1,0:T(4,128)}, f32[10,8,4,512]{3,2,1,0:T(4,128)}) custom-call(f32[10,8,4,512]{3,2,1,0:T(4,128)S(1)} %get-tuple-element.4.relaxed, f32[10,8,4,512]{3,2,1,0:T(4,128)S(1)} %get-tuple-element.5.residual), custom_call_target="tpu_custom_call" | custom-call | tf_op jit(solution)/shard_map/pallas_call | solution.py:693

commit v3 on v2

--- a/solution.py
+++ b/solution.py
@@ -115,6 +115,8 @@
     second_in,
     packed,
     ghosts,
+    face_tile,
+    face_shift,
     load_sem,
     all_send,
     all_recv,
@@ -144,7 +146,7 @@
         )
         return carry
 
-    lax.fori_loop(0, n - 1, greet, 0)
+    lax.fori_loop(0, n - 1, greet, 0, unroll=True)
 
     def load(i, src, dst):
         return pltpu.make_async_copy(src, dst, load_sem.at[i])
@@ -316,20 +318,26 @@
     angle = jnp.broadcast_to(phase_ref[0], (8, 128))
     cos_value, sin_value = jnp.cos(angle), jnp.sin(angle)
 
-    def make_inflow(strips):
-        def body(a, acc):
+    def name_faces():
+        def body(face, carry):
+            owner, slot = owner_ref[face], slot_ref[face]
+            side, line = face // (AX * RD), face % (AX * RD)
+            face_tile[face] = owner % wide * nz + owner // wide
+            face_shift[face] = 2 * (line - slot) + 1 - 2 * side + 128
+            return carry
+
+        lax.fori_loop(0, 2 * AX * RD, body, 0, unroll=True)
+
+    def make_inflow(strips, stations):
+        partner = jnp.zeros((8, 128), F32)
+        for a in stations:
             for side in range(2):
                 for r in range(RD):
                     face = side * AX * RD + a * RD + r
-                    owner = owner_ref[face]
-                    slot = slot_ref[face]
-                    entry = strips[owner % wide * nz + owner // wide]
-                    to = a * 8 + 2 * r + 1 - side
-                    moved = pltpu.roll(entry, to - (slot * 2 + side) + 128, 1)
-                    acc = jnp.where(lane8 % 64 == to, moved, acc)
-            return acc
-
-        partner = lax.fori_loop(0, AX, body, jnp.zeros((8, 128), F32), unroll=True)
+                    entry = strips[face_tile[face]]
+                    moved = pltpu.roll(entry, face_shift[face], 1)
+                    here = lane8 % 64 == a * 8 + 2 * r + 1 - side
+                    partner = jnp.where(here, moved, partner)
         other = rolled(partner, 64)
         plus = (lane8 < 64) == (lane8 % 2 == 1)
         flow = cos_value * partner + jnp.where(plus, sin_value, -sin_value) * other
@@ -375,8 +383,8 @@
 
         lax.fori_loop(0, RD, body, 0)
 
-    def add_inflow(strips, dst, first, scale):
-        flow = scale * make_inflow(strips)
+    def add_inflow(strips, dst, first, scale, stations):
+        flow = scale * make_inflow(strips, stations)
         last = dst.shape[0] - 1
 
         def body(r, carry):
@@ -485,6 +493,8 @@
                 put(dst, rows, get(dst, rows) + scale * ghost)
 
     seventh = 1.0 / 7.0
+    middle = range(1, AX - 1)
+    ends = (0, AX - 1)
     loads[0].wait()
     spread(stage, s0, OWN)
     for s in (s0, s1):
@@ -515,19 +525,14 @@
     gain_rows[:, :128] = jnp.concatenate(rows0, axis=0).T
     gain_rows[:, 128:] = jnp.concatenate(rows1, axis=0).T
     loads[5].wait()
+    name_faces()
 
     pl.semaphore_wait(barrier, n - 1)
     strip_z(0, strips0)
+    exchange(0, modes_out, modes_in)
     halo0 = line_halo(0, s0)
     halo_start(halo0)
-    exchange(0, modes_out, modes_in)
     strip_w(0, strips0)
-
-    def emit_base(at, mine, value):
-        put(s1, pl.ds(OWN + at, 8), mine + value * seventh)
-
-    halo_recv_wait(halo0)
-    sweep(s0, emit_base)
 
     exchange_wait(0, modes_in)
     first = filtered([modes_in[pl.ds(f, n, stride=8), :] for f in range(5)])
@@ -535,10 +540,17 @@
         first_out[pl.ds(g, n, stride=8), :] = first[g]
     exchange(2, first_out, first_in)
 
+    def emit_base(at, mine, value):
+        put(s1, pl.ds(OWN + at, 8), mine + value * seventh)
+
+    halo_recv_wait(halo0)
+    sweep(s0, emit_base)
+
     strip_wait(0, strips0)
-    add_inflow(strips0, s1, OWN, seventh)
+    add_inflow(strips0, s1, OWN, seventh, ends)
     forward(s1, late_out)
     exchange(1, late_out, late_in)
+    add_inflow(strips0, s1, OWN, seventh, middle)
 
     exchange_wait(2, first_in)
     inverse(first_in)
@@ -571,7 +583,7 @@
     halo_recv_wait(halo1)
     sweep(s1, emit_residual)
     strip_wait(1, strips1)
-    add_inflow(strips1, res, 0, 1.0)
+    add_inflow(strips1, res, 0, 1.0, range(AX))
 
     def relax(i, carry):
         at = pl.multiple_of(i * 16, 8)
@@ -580,7 +592,6 @@
         return carry
 
     lax.fori_loop(0, RD * LINE // 16, relax, 0, unroll=4)
-    middle = range(1, AX - 1)
     collect(res, residual, middle)
     collect(source, relaxed, middle)
 
@@ -593,7 +604,6 @@
         return carry
 
     lax.fori_loop(0, RD, last_ghosts, 0, unroll=True)
-    ends = (0, AX - 1)
     collect(res, residual, ends)
     collect(source, relaxed, ends)
 
@@ -665,6 +675,8 @@
             *[vmem(peers, F32) for _ in range(8)],
             vmem((2, rad, 128), F32),
             vmem((azi // 128, RD * 32, 128), F32),
+            pltpu.SMEM((2 * AX * RD,), jnp.int32),
+            pltpu.SMEM((2 * AX * RD,), jnp.int32),
             pltpu.SemaphoreType.DMA((6,)),
             pltpu.SemaphoreType.DMA((4,)),
             pltpu.SemaphoreType.DMA((4,)),

time: 50.3 us -> 48.2 us (0.958)
  Pallas kernels: 48.2 us -> 46.1 us
    pallas_call x1, Pallas kernels: 47.1 us -> 45 us  [on_device(): pl.pallas_call(functools.partial(kernel, n, 8 if n >= 64 else 4), out_sha...]
where the time goes in v3:
time: 48.2 us; the launch traced here: 48 us
  Pallas kernels  46.1 us (96%)
  between operations  1.93 us (4%)
    pallas_call x1, Pallas kernels, on_device(): pl.pallas_call(functools.partial(kernel, n, 8 if n >= 64 else 4), out_sha...  45 us
    pallas_call x1, Pallas kernels, on_device(): pl.pallas_call(write_kernel, out_shape=(jax.ShapeDtypeStruct(shape, F32),...  1.07 us

profile of v3, /device:TPU:1, one launch (start us, length us, event | category | flops | bytes accessed | tf_op | source)
XLA Modules:
  0.0 48.0 jit_solution(16308666036029010541)
XLA Ops:
  1.9 45.0 %shard_map.131 = (f32[10,8,4,512]{3,2,1,0:T(4,128)S(1)}, f32[10,8,4,512]{3,2,1,0:T(4,128)S(1)}) custom-call(f32[10,8,4,512]{3,2,1,0:T(4,128)} %state_hbm.1, f32[10,8,4,512]{3,2,1,0:T(4,128)} %source_hbm.1, f32[2,5,8,256]{3,2,1,0:T(8,128)} %bitcast.3, f32[256,256]{1,0:T(8,128)} %basis_hbm.1, bf16[2,4,128,256]{3,2,1,0:T(8,128)(2,1)} %constant.4.clone.ahead_hbm, ...), custom_call_target="tpu_custom_call" | custom-call | tf_op jit(solution)/shard_map/pallas_call | solution.py:652
  47.0 1.1 %shard_map.132 = (f32[10,8,4,512]{3,2,1,0:T(4,128)}, f32[10,8,4,512]{3,2,1,0:T(4,128)}) custom-call(f32[10,8,4,512]{3,2,1,0:T(4,128)S(1)} %get-tuple-element.4.relaxed, f32[10,8,4,512]{3,2,1,0:T(4,128)S(1)} %get-tuple-element.5.residual), custom_call_target="tpu_custom_call" | custom-call | tf_op jit(solution)/shard_map/pallas_call | solution.py:705

commit v4 on v3

--- a/solution.py
+++ b/solution.py
@@ -287,7 +287,7 @@
                 staged[cf, a] = get(src, pl.ds(cf * 8 + a, RD, stride=LINE))
             return carry
 
-        lax.fori_loop(0, 10, body, 0)
+        lax.fori_loop(0, 10, body, 0, unroll=True)
 
     group8 = lane8 // 8 % 8
 
@@ -617,10 +617,13 @@
 
 
 def write_kernel(relaxed, residual, relaxed_hbm, residual_hbm, sem):
-    copies = [
-        pltpu.make_async_copy(relaxed, relaxed_hbm, sem.at[0]),
-        pltpu.make_async_copy(residual, residual_hbm, sem.at[1]),
-    ]
+    copies = []
+    for part in range(5):
+        fields = pl.ds(2 * part, 2)
+        for i, (src, dst) in enumerate(((relaxed, relaxed_hbm), (residual, residual_hbm))):
+            copies.append(
+                pltpu.make_async_copy(src.at[fields], dst.at[fields], sem.at[2 * part + i])
+            )
     for copy in copies:
         copy.start()
     for copy in copies:
@@ -707,7 +710,7 @@
         out_shape=(jax.ShapeDtypeStruct(shape, F32), jax.ShapeDtypeStruct(shape, F32)),
         in_specs=[hbm, hbm],
         out_specs=(hbm, hbm),
-        scratch_shapes=[pltpu.SemaphoreType.DMA((2,))],
+        scratch_shapes=[pltpu.SemaphoreType.DMA((10,))],
         compiler_params=pltpu.CompilerParams(vmem_limit_bytes=4 * 1024 * 1024),
     )(relaxed, residual)
 

time: 48.2 us -> 48.1 us (level)
  no operation moved by 1% of the time
where the time goes in v4:
time: 48.1 us; the launch traced here: 47.9 us
  Pallas kernels  46 us (96%)
  between operations  1.93 us (4%)
    pallas_call x1, Pallas kernels, on_device(): pl.pallas_call(functools.partial(kernel, n, 8 if n >= 64 else 4), out_sha...  44.9 us
    pallas_call x1, Pallas kernels, on_device(): pl.pallas_call(write_kernel, out_shape=(jax.ShapeDtypeStruct(shape, F32),...  1.13 us

profile of v4, /device:TPU:1, one launch (start us, length us, event | category | flops | bytes accessed | tf_op | source)
XLA Modules:
  0.0 47.9 jit_solution(13884345167729358244)
XLA Ops:
  1.9 44.9 %shard_map.131 = (f32[10,8,4,512]{3,2,1,0:T(4,128)S(1)}, f32[10,8,4,512]{3,2,1,0:T(4,128)S(1)}) custom-call(f32[10,8,4,512]{3,2,1,0:T(4,128)} %state_hbm.1, f32[10,8,4,512]{3,2,1,0:T(4,128)} %source_hbm.1, f32[2,5,8,256]{3,2,1,0:T(8,128)} %bitcast.3, f32[256,256]{1,0:T(8,128)} %basis_hbm.1, bf16[2,4,128,256]{3,2,1,0:T(8,128)(2,1)} %constant.4.clone.ahead_hbm, ...), custom_call_target="tpu_custom_call" | custom-call | tf_op jit(solution)/shard_map/pallas_call | solution.py:655
  46.8 1.1 %shard_map.132 = (f32[10,8,4,512]{3,2,1,0:T(4,128)}, f32[10,8,4,512]{3,2,1,0:T(4,128)}) custom-call(f32[10,8,4,512]{3,2,1,0:T(4,128)S(1)} %get-tuple-element.4.relaxed, f32[10,8,4,512]{3,2,1,0:T(4,128)S(1)} %get-tuple-element.5.residual), custom_call_target="tpu_custom_call" | custom-call | tf_op jit(solution)/shard_map/pallas_call | solution.py:708
